TPU v7x, 128 devices: a whole 4x4x4 slice. The times are simulated.
128 devices in a mesh: gx: 8 (over x, core), gy: 16 (over y, z).
Axes of the slice: x: 4, y: 4, z: 4, core: 2. Of those that a mesh axis runs over, the one named last changes fastest.
Arguments:
- pressure_source: float32 [192, 384, 384], P('gx', 'gy'), may hold values from -6 to 6
- building_heights: int32 [32, 64], replicated, may hold values from 0 to 63
Outputs:
- correction: float32 [192, 384, 384], P('gx', 'gy')
- coarse_solution: float32 [64, 128, 128], P('gx', 'gy')
Inputs may be any that keep to these rules, and one draw needn't show every extreme that they name: `building_heights`: the height of the building in each element column, in elements, so that the top layer of every column is fluid.
All inputs are finite; a program needn't handle non-finite values.
Results may differ from a plain program's by a relative error of at most 0.0003.
Values sent between devices are 32-bit elements; how exact they have to be, the bound alone decides.
No kernel may reach another device: no remote copies, remote signals or barrier semaphores. Data moves between devices by JAX's collectives and lax.ppermute only.
A program may use at most 128 MiB of HBM per device.

v0:
```python
import jax
import jax.numpy as jnp
import numpy as np
from jax import lax
from jax.sharding import PartitionSpec as P

CG_ITERS = 10
HIGHEST = lax.Precision.HIGHEST


def with_halo(cells, sides, width):
    for axis, dim in sides:
        count = lax.axis_size(axis)
        ends = count - 1
        head = lax.slice_in_dim(cells, 0, width, axis=dim)
        tail = lax.slice_in_dim(cells, cells.shape[dim] - width, cells.shape[dim], axis=dim)
        cells = jnp.concatenate(
            [
                lax.ppermute(tail, axis, [(i, (i + 1) % count) for i in range(ends)]),
                cells,
                lax.ppermute(head, axis, [((i + 1) % count, i) for i in range(ends)]),
            ],
            axis=dim,
        )
    return cells


def gll_nodes(node_count):
    if node_count == 6:
        outer_point = 0.7650553239294647
        inner_point = 0.2852315164806451
        points = [-1.0, -outer_point, -inner_point, inner_point, outer_point, 1.0]
        weights = [
            1.0 / 15.0,
            0.378474956297847,
            0.5548583770354863,
            0.5548583770354863,
            0.378474956297847,
            1.0 / 15.0,
        ]
    elif node_count == 4:
        inner_point = 0.4472135954999579
        points = [-1.0, -inner_point, inner_point, 1.0]
        weights = [1.0 / 6.0, 5.0 / 6.0, 5.0 / 6.0, 1.0 / 6.0]
    else:
        points = [-1.0, 1.0]
        weights = [1.0, 1.0]
    return (np.array(points), np.array(weights))


def diagonal_of(matrix):
    return np.array([matrix[index_id, index_id] for index_id in range(matrix.shape[0])])


def lagrange_tables(node_count):
    points, weights = gll_nodes(node_count)
    others = [
        [points[col_id] - points[other] for other in range(node_count) if other != col_id]
        for col_id in range(node_count)
    ]
    bary_weights = np.array([1.0 / np.prod(entries) for entries in others])
    derivative = np.zeros((node_count, node_count))
    for row_id in range(node_count):
        for col_id in range(node_count):
            if row_id != col_id:
                derivative[row_id, col_id] = (
                    bary_weights[col_id] / bary_weights[row_id] / (points[row_id] - points[col_id])
                )
        derivative[row_id, row_id] = -np.sum(derivative[row_id])
    stiffness = derivative.T @ (weights[:, None] * derivative)
    return (stiffness, weights)


def interpolation(coarse_count, fine_count):
    coarse_points = gll_nodes(coarse_count)[0]
    fine_points = gll_nodes(fine_count)[0]
    matrix = np.ones((fine_count, coarse_count))
    for row_id in range(fine_count):
        for col_id in range(coarse_count):
            for other in range(coarse_count):
                if other != col_id:
                    matrix[row_id, col_id] *= (fine_points[row_id] - coarse_points[other]) / (
                        coarse_points[col_id] - coarse_points[other]
                    )
    return matrix


def chebyshev_bounds(node_count):
    stiffness, weights = lagrange_tables(node_count)
    row_abs = np.abs(stiffness).sum(axis=1)
    diag_vals = diagonal_of(stiffness)
    wide_one = weights[:, None, None]
    wide_two = weights[None, :, None]
    wide_three = weights[None, None, :]
    numerator = (
        row_abs[:, None, None] * wide_two * wide_three
        + wide_one * row_abs[None, :, None] * wide_three
        + wide_one * wide_two * row_abs[None, None, :]
    )
    denominator = (
        diag_vals[:, None, None] * wide_two * wide_three
        + wide_one * diag_vals[None, :, None] * wide_three
        + wide_one * wide_two * diag_vals[None, None, :]
    )
    top_bound = float(np.max(numerator / denominator))
    return (top_bound, 0.1 * top_bound)


def tiled(vector, length, position):
    repeated = jnp.asarray(np.tile(vector, length // vector.shape[0]), jnp.float32)
    return repeated.reshape(tuple((length if axis_id == position else 1 for axis_id in range(3))))


def along_first(values, matrix):
    out_count, in_count = matrix.shape
    blocks = values.shape[0] // in_count
    shaped = values.reshape(blocks, in_count, values.shape[1] * values.shape[2])
    result = jnp.einsum("ip,xpr->xir", jnp.asarray(matrix, jnp.float32), shaped, precision=HIGHEST)
    return result.reshape(blocks * out_count, values.shape[1], values.shape[2])


def along_second(values, matrix):
    out_count, in_count = matrix.shape
    blocks = values.shape[1] // in_count
    shaped = values.reshape(values.shape[0], blocks, in_count, values.shape[2])
    result = jnp.einsum(
        "jq,xyqc->xyjc", jnp.asarray(matrix, jnp.float32), shaped, precision=HIGHEST
    )
    return result.reshape(values.shape[0], blocks * out_count, values.shape[2])


def along_third(values, matrix):
    out_count, in_count = matrix.shape
    blocks = values.shape[2] // in_count
    block_matrix = jnp.asarray(np.kron(np.eye(blocks), matrix.T), jnp.float32)
    result = jnp.dot(values.reshape(-1, values.shape[2]), block_matrix, precision=HIGHEST)
    return result.reshape(values.shape[0], values.shape[1], blocks * out_count)


def pass_first(padded, node_count):
    position = np.arange(padded.shape[0] - 2) % node_count
    at_start = jnp.asarray(position == 0, jnp.float32)[:, None, None]
    at_end = jnp.asarray(position == node_count - 1, jnp.float32)[:, None, None]
    return padded[1:-1] + at_start * padded[:-2] + at_end * padded[2:]


def pass_second(padded, node_count):
    position = np.arange(padded.shape[1] - 2) % node_count
    at_start = jnp.asarray(position == 0, jnp.float32)[None, :, None]
    at_end = jnp.asarray(position == node_count - 1, jnp.float32)[None, :, None]
    return padded[:, 1:-1] + at_start * padded[:, :-2] + at_end * padded[:, 2:]


def pass_third(values, node_count):
    position = np.arange(values.shape[2]) % node_count
    at_start = jnp.asarray(position == 0, jnp.float32)[None, None, :]
    at_end = jnp.asarray(position == node_count - 1, jnp.float32)[None, None, :]
    earlier = jnp.pad(values[:, :, :-1], ((0, 0), (0, 0), (1, 0)))
    following = jnp.pad(values[:, :, 1:], ((0, 0), (0, 0), (0, 1)))
    return values + at_start * earlier + at_end * following


def rim_joint(values):
    return with_halo(values, (("gx", 0), ("gy", 1)), 1)


def assemble(values, node_count):
    summed = pass_third(values, node_count)
    padded = rim_joint(summed)
    return pass_second(pass_first(padded, node_count), node_count)


def spread_counts(elem_pad, node_count):
    position = np.arange(node_count)
    at_start = jnp.asarray(position == 0, jnp.float32)
    at_end = jnp.asarray(position == node_count - 1, jnp.float32)
    step_one = (
        elem_pad[1:-1][:, None]
        + at_start[None, :, None, None] * elem_pad[:-2][:, None]
        + at_end[None, :, None, None] * elem_pad[2:][:, None]
    )
    step_one = step_one.reshape(-1, elem_pad.shape[1], elem_pad.shape[2])
    step_two = (
        step_one[:, 1:-1][:, :, None]
        + at_start[None, None, :, None] * step_one[:, :-2][:, :, None]
        + at_end[None, None, :, None] * step_one[:, 2:][:, :, None]
    )
    step_two = step_two.reshape(step_one.shape[0], -1, elem_pad.shape[2])
    step_three = (
        step_two[:, :, 1:-1][:, :, :, None]
        + at_start * step_two[:, :, :-2][:, :, :, None]
        + at_end * step_two[:, :, 2:][:, :, :, None]
    )
    return step_three.reshape(step_two.shape[0], step_two.shape[1], -1)


def level_data(fluid_pad, exist_pad, node_count):
    fluid_count = spread_counts(fluid_pad, node_count)
    exist_count = spread_counts(exist_pad, node_count)
    ground = jnp.asarray(np.arange(fluid_count.shape[2]) > 0, jnp.float32)[None, None, :]
    node_mask = (
        (fluid_count == exist_count).astype(jnp.float32)
        * (fluid_count > 0.5).astype(jnp.float32)
        * ground
    )
    node_weight = 1.0 / exist_count
    fluid_cells = fluid_pad[1:-1, 1:-1, 1:-1]
    fluid_node = jnp.repeat(
        jnp.repeat(jnp.repeat(fluid_cells, node_count, axis=0), node_count, axis=1),
        node_count,
        axis=2,
    )
    stiffness, weights = lagrange_tables(node_count)
    stiff_diag = diagonal_of(stiffness)
    dims_now = fluid_count.shape
    local_diag = (
        tiled(stiff_diag, dims_now[0], 0)
        * tiled(weights, dims_now[1], 1)
        * tiled(weights, dims_now[2], 2)
    )
    local_diag = local_diag + tiled(weights, dims_now[0], 0) * tiled(
        stiff_diag, dims_now[1], 1
    ) * tiled(weights, dims_now[2], 2)
    local_diag = local_diag + tiled(weights, dims_now[0], 0) * tiled(
        weights, dims_now[1], 1
    ) * tiled(stiff_diag, dims_now[2], 2)
    inverse_diag = node_mask / (fluid_count * local_diag + 1.0 - node_mask)
    return (node_count, fluid_node, node_mask, node_weight, inverse_diag)


def element_action(values, level_info):
    node_count, fluid_node = (level_info[0], level_info[1])
    stiffness, weights = lagrange_tables(node_count)
    mass_first = tiled(weights, values.shape[0], 0)
    mass_second = tiled(weights, values.shape[1], 1)
    mass_third = tiled(weights, values.shape[2], 2)
    summed_terms = mass_second * mass_third * along_first(values, stiffness)
    summed_terms = summed_terms + mass_first * mass_third * along_second(values, stiffness)
    summed_terms = summed_terms + mass_first * mass_second * along_third(values, stiffness)
    return fluid_node * summed_terms


def apply_operator(values, level_info, assembler):
    return level_info[2] * assembler(element_action(values, level_info), level_info[0])


def smooth(target, start, level_info, bounds, assembler, from_zero):
    top_bound, low_bound = bounds
    center = 0.5 * (top_bound + low_bound)
    half_width = 0.5 * (top_bound - low_bound)
    inverse_diag = level_info[4]
    if from_zero:
        residual_now = target
        update = inverse_diag * residual_now / center
        solution = update
    else:
        residual_now = target - apply_operator(start, level_info, assembler)
        update = inverse_diag * residual_now / center
        solution = start + update
    residual_now = residual_now - apply_operator(update, level_info, assembler)
    rho_first = half_width / center
    rho_next = 1.0 / (2.0 * center / half_width - rho_first)
    update = (
        rho_next * rho_first * update + 2.0 * rho_next / half_width * inverse_diag * residual_now
    )
    return solution + update


def restrict(values, coarse_count, fine_count):
    matrix = interpolation(coarse_count, fine_count).T
    return along_third(along_second(along_first(values, matrix), matrix), matrix)


def prolong(values, coarse_count, fine_count):
    matrix = interpolation(coarse_count, fine_count)
    return along_third(along_second(along_first(values, matrix), matrix), matrix)


def conjugate_gradients(target, level_info, assembler, reduce_sum):
    node_weight = level_info[3]
    norm_start = reduce_sum(jnp.sum(node_weight * target * target))

    def iterate(index, cg_state):
        solution, residual_now, direction, norm_now = cg_state
        applied = apply_operator(direction, level_info, assembler)
        step_len = norm_now / reduce_sum(jnp.sum(node_weight * direction * applied))
        solution = solution + step_len * direction
        residual_now = residual_now - step_len * applied
        norm_next = reduce_sum(jnp.sum(node_weight * residual_now * residual_now))
        direction = residual_now + norm_next / norm_now * direction
        return (solution, residual_now, direction, norm_next)

    final_state = lax.fori_loop(
        0, CG_ITERS, iterate, (jnp.zeros_like(target), target, target, norm_start)
    )
    return final_state[0]


def sum_spread(partial_sum):
    return lax.psum(partial_sum, ("gx", "gy"))


def coarse_spread(target, level_info):
    return conjugate_gradients(target, level_info, assemble, sum_spread)


def per_device(pressure_source, building_heights):
    side_first = pressure_source.shape[0] // 6
    side_second = pressure_source.shape[1] // 6
    column = pressure_source.shape[2] // 6
    start_first = lax.axis_index("gx") * side_first
    start_second = lax.axis_index("gy") * side_second
    heights_pad = jnp.pad(building_heights, 1, constant_values=column)
    local_heights = lax.dynamic_slice(
        heights_pad, (start_first, start_second), (side_first + 2, side_second + 2)
    )
    exist_cols = lax.dynamic_slice(
        jnp.pad(jnp.ones(building_heights.shape, jnp.float32), 1),
        (start_first, start_second),
        (side_first + 2, side_second + 2),
    )
    layers = jnp.arange(-1, column + 1, dtype=jnp.int32)
    inside = ((layers >= 0) & (layers < column)).astype(jnp.float32)[None, None, :]
    fluid_pad = (layers[None, None, :] >= local_heights[:, :, None]).astype(jnp.float32) * inside
    exist_pad = exist_cols[:, :, None] * inside
    fine_level = level_data(fluid_pad, exist_pad, 6)
    middle_level = level_data(fluid_pad, exist_pad, 4)
    coarse_level = level_data(fluid_pad, exist_pad, 2)
    fine_bounds = chebyshev_bounds(6)
    middle_bounds = chebyshev_bounds(4)
    target_fine = fine_level[2] * assemble(pressure_source, 6)
    fine_sol = smooth(target_fine, None, fine_level, fine_bounds, assemble, True)
    fine_res = target_fine - apply_operator(fine_sol, fine_level, assemble)
    target_middle = middle_level[2] * assemble(restrict(fine_level[3] * fine_res, 4, 6), 4)
    middle_sol = smooth(target_middle, None, middle_level, middle_bounds, assemble, True)
    middle_res = target_middle - apply_operator(middle_sol, middle_level, assemble)
    target_coarse = coarse_level[2] * assemble(restrict(middle_level[3] * middle_res, 2, 4), 2)
    coarse_sol = coarse_spread(target_coarse, coarse_level)
    middle_sol = middle_sol + middle_level[2] * prolong(coarse_sol, 2, 4)
    middle_sol = smooth(target_middle, middle_sol, middle_level, middle_bounds, assemble, False)
    fine_sol = fine_sol + fine_level[2] * prolong(middle_sol, 4, 6)
    fine_sol = smooth(target_fine, fine_sol, fine_level, fine_bounds, assemble, False)
    return (fine_sol, coarse_sol)


def solution(mesh):
    in_specs = (P("gx", "gy", None), P())
    out_specs = (P("gx", "gy", None), P("gx", "gy", None))
    return jax.shard_map(
        per_device, mesh=mesh, in_specs=in_specs, out_specs=out_specs, check_vma=False
    )
```

profile of v0, /device:TPU:105, one launch (start us, length us, event | category | flops | bytes accessed | tf_op | source)
XLA Modules:
  0.0 2164.7 jit_solution(11092381032411942674)
XLA Ops:
  2.9 3.7 collective-permute-start.4
  22.5 4.6 copy.272
  30.0 4.7 copy.273
  37.5 4.7 copy.275
  45.0 4.7 copy.281
  52.5 4.6 copy.282
  59.9 4.7 copy.284
  68.9 3.9 copy.291
  93.2 4.2 collective-permute-start.8
  102.8 3.9 collective-permute-start.10
  109.8 3.8 collective-permute-done.11
  129.4 3.6 collective-permute-start.12
  170.7 3.8 collective-permute-start.19
  242.8 4.0 collective-permute-start.22
  266.6 3.4 collective-permute-start.24
  275.1 5.7 collective-permute-start.26
  283.5 3.9 collective-permute-done.27
  328.0 63.3 %psum.27 = f32[]{:T(128)} all-reduce(f32[]{:T(128)} %get-tuple-element.560), channel_id=1, replica_groups=mesh['gx'=8,'gy'=16] {'gx','gy'}, use_global_device_ids=true, to_apply=%region_1.2 | all-reduce | flops 1 | bytes 8 | tf_op jit(solution)/shard_map/psum | solution.py:300
  391.3 1636.0 %while.23 = (s32[]{:T(128)}, f32[8,8,128]{2,1,0:T(8,128)}, f32[8,8,128]{2,1,0:T(8,128)}, f32[8,8,128]{2,1,0:T(8,128)S(1)}, f32[]{:T(128)}, /*index=5*/f32[8,8,64...) while((s32[]{:T(128)}, f32[8,8,128]{2,1,0:T(8,128)}, ...), condition=%wide.region_7.8_spmd.clone.clone.clone.clone.clone, body=%wide.region_2.7_spmd.sunk.clone.clone.clone.clone.clone.sunk | while | flops 13401093 | bytes 2653795 | solution.py:293
  398.9 3.5 collective-permute-start.1
  405.7 5.5 collective-permute-start.3
  424.1 63.5 %psum.42 = f32[]{:T(128)} all-reduce(f32[]{:T(128)} %get-tuple-element.823), channel_id=1, replica_groups=mesh['gx'=8,'gy'=16] {'gx','gy'}, use_global_device_ids=true, to_apply=%region_4.4 | all-reduce | flops 1 | bytes 8 | tf_op jit(solution)/shard_map/while/body/eval_jaxpr/psum | solution.py:300
  490.4 62.5 %psum.43 = f32[]{:T(128)} all-reduce(f32[]{:T(128)} %get-tuple-element.825), channel_id=1, replica_groups=mesh['gx'=8,'gy'=16] {'gx','gy'}, use_global_device_ids=true, to_apply=%region_6.6 | all-reduce | flops 1 | bytes 8 | tf_op jit(solution)/shard_map/while/body/eval_jaxpr/psum | solution.py:300
  570.0 4.5 collective-permute-start.3
  587.4 63.8 %psum.42 = f32[]{:T(128)} all-reduce(f32[]{:T(128)} %get-tuple-element.823), channel_id=1, replica_groups=mesh['gx'=8,'gy'=16] {'gx','gy'}, use_global_device_ids=true, to_apply=%region_4.4 | all-reduce | flops 1 | bytes 8 | tf_op jit(solution)/shard_map/while/body/eval_jaxpr/psum | solution.py:300
  653.9 62.5 %psum.43 = f32[]{:T(128)} all-reduce(f32[]{:T(128)} %get-tuple-element.825), channel_id=1, replica_groups=mesh['gx'=8,'gy'=16] {'gx','gy'}, use_global_device_ids=true, to_apply=%region_6.6 | all-reduce | flops 1 | bytes 8 | tf_op jit(solution)/shard_map/while/body/eval_jaxpr/psum | solution.py:300
  726.0 3.5 collective-permute-start.1
  733.6 4.7 collective-permute-start.3
  751.2 63.5 %psum.42 = f32[]{:T(128)} all-reduce(f32[]{:T(128)} %get-tuple-element.823), channel_id=1, replica_groups=mesh['gx'=8,'gy'=16] {'gx','gy'}, use_global_device_ids=true, to_apply=%region_4.4 | all-reduce | flops 1 | bytes 8 | tf_op jit(solution)/shard_map/while/body/eval_jaxpr/psum | solution.py:300
  817.5 62.5 %psum.43 = f32[]{:T(128)} all-reduce(f32[]{:T(128)} %get-tuple-element.825), channel_id=1, replica_groups=mesh['gx'=8,'gy'=16] {'gx','gy'}, use_global_device_ids=true, to_apply=%region_6.6 | all-reduce | flops 1 | bytes 8 | tf_op jit(solution)/shard_map/while/body/eval_jaxpr/psum | solution.py:300
  889.6 3.5 collective-permute-start.1
  897.2 4.7 collective-permute-start.3
  914.8 63.6 %psum.42 = f32[]{:T(128)} all-reduce(f32[]{:T(128)} %get-tuple-element.823), channel_id=1, replica_groups=mesh['gx'=8,'gy'=16] {'gx','gy'}, use_global_device_ids=true, to_apply=%region_4.4 | all-reduce | flops 1 | bytes 8 | tf_op jit(solution)/shard_map/while/body/eval_jaxpr/psum | solution.py:300
  981.1 62.5 %psum.43 = f32[]{:T(128)} all-reduce(f32[]{:T(128)} %get-tuple-element.825), channel_id=1, replica_groups=mesh['gx'=8,'gy'=16] {'gx','gy'}, use_global_device_ids=true, to_apply=%region_6.6 | all-reduce | flops 1 | bytes 8 | tf_op jit(solution)/shard_map/while/body/eval_jaxpr/psum | solution.py:300
  1053.2 3.5 collective-permute-start.1
  1060.8 4.7 collective-permute-start.3
  1078.4 63.6 %psum.42 = f32[]{:T(128)} all-reduce(f32[]{:T(128)} %get-tuple-element.823), channel_id=1, replica_groups=mesh['gx'=8,'gy'=16] {'gx','gy'}, use_global_device_ids=true, to_apply=%region_4.4 | all-reduce | flops 1 | bytes 8 | tf_op jit(solution)/shard_map/while/body/eval_jaxpr/psum | solution.py:300
  1144.7 62.5 %psum.43 = f32[]{:T(128)} all-reduce(f32[]{:T(128)} %get-tuple-element.825), channel_id=1, replica_groups=mesh['gx'=8,'gy'=16] {'gx','gy'}, use_global_device_ids=true, to_apply=%region_6.6 | all-reduce | flops 1 | bytes 8 | tf_op jit(solution)/shard_map/while/body/eval_jaxpr/psum | solution.py:300
  1216.8 3.5 collective-permute-start.1
  1224.3 4.7 collective-permute-start.3
  1242.0 63.6 %psum.42 = f32[]{:T(128)} all-reduce(f32[]{:T(128)} %get-tuple-element.823), channel_id=1, replica_groups=mesh['gx'=8,'gy'=16] {'gx','gy'}, use_global_device_ids=true, to_apply=%region_4.4 | all-reduce | flops 1 | bytes 8 | tf_op jit(solution)/shard_map/while/body/eval_jaxpr/psum | solution.py:300
  1308.3 62.5 %psum.43 = f32[]{:T(128)} all-reduce(f32[]{:T(128)} %get-tuple-element.825), channel_id=1, replica_groups=mesh['gx'=8,'gy'=16] {'gx','gy'}, use_global_device_ids=true, to_apply=%region_6.6 | all-reduce | flops 1 | bytes 8 | tf_op jit(solution)/shard_map/while/body/eval_jaxpr/psum | solution.py:300
  1380.4 3.5 collective-permute-start.1
  1387.9 4.7 collective-permute-start.3
  1405.6 63.6 %psum.42 = f32[]{:T(128)} all-reduce(f32[]{:T(128)} %get-tuple-element.823), channel_id=1, replica_groups=mesh['gx'=8,'gy'=16] {'gx','gy'}, use_global_device_ids=true, to_apply=%region_4.4 | all-reduce | flops 1 | bytes 8 | tf_op jit(solution)/shard_map/while/body/eval_jaxpr/psum | solution.py:300
  1471.8 62.5 %psum.43 = f32[]{:T(128)} all-reduce(f32[]{:T(128)} %get-tuple-element.825), channel_id=1, replica_groups=mesh['gx'=8,'gy'=16] {'gx','gy'}, use_global_device_ids=true, to_apply=%region_6.6 | all-reduce | flops 1 | bytes 8 | tf_op jit(solution)/shard_map/while/body/eval_jaxpr/psum | solution.py:300
  1544.0 3.5 collective-permute-start.1
  1551.5 4.7 collective-permute-start.3
  1569.2 63.6 %psum.42 = f32[]{:T(128)} all-reduce(f32[]{:T(128)} %get-tuple-element.823), channel_id=1, replica_groups=mesh['gx'=8,'gy'=16] {'gx','gy'}, use_global_device_ids=true, to_apply=%region_4.4 | all-reduce | flops 1 | bytes 8 | tf_op jit(solution)/shard_map/while/body/eval_jaxpr/psum | solution.py:300
  1635.4 62.5 %psum.43 = f32[]{:T(128)} all-reduce(f32[]{:T(128)} %get-tuple-element.825), channel_id=1, replica_groups=mesh['gx'=8,'gy'=16] {'gx','gy'}, use_global_device_ids=true, to_apply=%region_6.6 | all-reduce | flops 1 | bytes 8 | tf_op jit(solution)/shard_map/while/body/eval_jaxpr/psum | solution.py:300
  1707.6 3.5 collective-permute-start.1
  1715.1 4.7 collective-permute-start.3
  1732.7 63.6 %psum.42 = f32[]{:T(128)} all-reduce(f32[]{:T(128)} %get-tuple-element.823), channel_id=1, replica_groups=mesh['gx'=8,'gy'=16] {'gx','gy'}, use_global_device_ids=true, to_apply=%region_4.4 | all-reduce | flops 1 | bytes 8 | tf_op jit(solution)/shard_map/while/body/eval_jaxpr/psum | solution.py:300
  1799.0 62.5 %psum.43 = f32[]{:T(128)} all-reduce(f32[]{:T(128)} %get-tuple-element.825), channel_id=1, replica_groups=mesh['gx'=8,'gy'=16] {'gx','gy'}, use_global_device_ids=true, to_apply=%region_6.6 | all-reduce | flops 1 | bytes 8 | tf_op jit(solution)/shard_map/while/body/eval_jaxpr/psum | solution.py:300
  1871.2 3.5 collective-permute-start.1
  1878.7 4.7 collective-permute-start.3
  1896.3 63.6 %psum.42 = f32[]{:T(128)} all-reduce(f32[]{:T(128)} %get-tuple-element.823), channel_id=1, replica_groups=mesh['gx'=8,'gy'=16] {'gx','gy'}, use_global_device_ids=true, to_apply=%region_4.4 | all-reduce | flops 1 | bytes 8 | tf_op jit(solution)/shard_map/while/body/eval_jaxpr/psum | solution.py:300
  1962.6 62.5 %psum.43 = f32[]{:T(128)} all-reduce(f32[]{:T(128)} %get-tuple-element.825), channel_id=1, replica_groups=mesh['gx'=8,'gy'=16] {'gx','gy'}, use_global_device_ids=true, to_apply=%region_6.6 | all-reduce | flops 1 | bytes 8 | tf_op jit(solution)/shard_map/while/body/eval_jaxpr/psum | solution.py:300
  2041.6 4.1 collective-permute-start.32
  2050.8 3.6 collective-permute-start.34
  2056.4 4.7 collective-permute-done.35
  2084.9 3.8 collective-permute-start.39
  2121.6 3.5 collective-permute-start.43
  2158.5 3.5 collective-permute-done.47
  (1127 shorter events, 639.8 us)
Async XLA Ops:
  2.9 9.5 collective-permute-start.4
  6.6 5.8 collective-permute-start.5
  13.1 59.8 %collective-permute-start.6 = (f32[26,1,384]{2,1,0:T(1,128)}, f32[26,1,384]{2,1,0:T(1,128)}, u32[]{:S(2)}, u32[]{:S(2)}) collective-permute-start(f32[26,1,384]{2,1,0:T(1,128)} %get-tuple-element.590), channel_id=1, source_target_pairs={{0,1},{1,2},{2,3},{3,4},{4,5},{5,6},{6,7},{7,8},{8,9},{9,10},{10,1... | collective-permute-start | bytes 119816 | tf_op jit(solution)/shard_map/ppermute | solution.py:19
  15.0 57.9 %collective-permute-start.7 = (f32[26,1,384]{2,1,0:T(1,128)}, f32[26,1,384]{2,1,0:T(1,128)}, u32[]{:S(2)}, u32[]{:S(2)}) collective-permute-start(f32[26,1,384]{2,1,0:T(1,128)} %get-tuple-element.591), channel_id=1, source_target_pairs={{1,0},{2,1},{3,2},{4,3},{5,4},{6,5},{7,6},{8,7},{9,8},{10,9},{11,1... | collective-permute-start | bytes 119816 | tf_op jit(solution)/shard_map/ppermute | solution.py:21
  93.2 6.2 collective-permute-start.8
  97.4 5.3 collective-permute-start.9
  102.8 7.0 collective-permute-start.10
  106.7 6.8 collective-permute-start.11
  129.4 6.4 collective-permute-start.12
  133.1 5.3 collective-permute-start.13
  138.4 6.1 collective-permute-start.14
  140.3 6.8 collective-permute-start.15
  168.8 49.5 %collective-permute-start.18 = (f32[18,1,256]{2,1,0:T(1,128)}, f32[18,1,256]{2,1,0:T(1,128)}, u32[]{:S(2)}, u32[]{:S(2)}) collective-permute-start(f32[18,1,256]{2,1,0:T(1,128)} %get-tuple-element.620), channel_id=1, source_target_pairs={{0,1},{1,2},{2,3},{3,4},{4,5},{5,6},{6,7},{7,8},{8,9},{9,10},{10,1... | collective-permute-start | bytes 55304 | tf_op jit(solution)/shard_map/ppermute | solution.py:19
  170.7 47.6 %collective-permute-start.19 = (f32[18,1,256]{2,1,0:T(1,128)}, f32[18,1,256]{2,1,0:T(1,128)}, u32[]{:S(2)}, u32[]{:S(2)}) collective-permute-start(f32[18,1,256]{2,1,0:T(1,128)} %get-tuple-element.621), channel_id=1, source_target_pairs={{1,0},{2,1},{3,2},{4,3},{5,4},{6,5},{7,6},{8,7},{9,8},{10,9},{11,1... | collective-permute-start | bytes 55304 | tf_op jit(solution)/shard_map/ppermute | solution.py:21
  233.3 8.7 collective-permute-start.20
  235.8 6.2 collective-permute-start.21
  242.8 11.7 collective-permute-start.22
  246.8 7.7 collective-permute-start.23
  266.6 5.4 collective-permute-start.24
  275.1 8.4 collective-permute-start.26
  280.8 6.6 collective-permute-start.27
  290.9 6.0 collective-permute-start.28
  299.8 23.9 %collective-permute-start.30 = (f32[10,1,128]{2,1,0:T(1,128)}, f32[10,1,128]{2,1,0:T(1,128)}, u32[]{:S(2)}, u32[]{:S(2)}) collective-permute-start(f32[10,1,128]{2,1,0:T(1,128)} %get-tuple-element.666), channel_id=1, source_target_pairs={{0,1},{1,2},{2,3},{3,4},{4,5},{5,6},{6,7},{7,8},{8,9},{9,10},{10,1... | collective-permute-start | bytes 15368 | tf_op jit(solution)/shard_map/ppermute | solution.py:19
  301.7 22.0 %collective-permute-start.31 = (f32[10,1,128]{2,1,0:T(1,128)}, f32[10,1,128]{2,1,0:T(1,128)}, u32[]{:S(2)}, u32[]{:S(2)}) collective-permute-start(f32[10,1,128]{2,1,0:T(1,128)} %get-tuple-element.667), channel_id=1, source_target_pairs={{1,0},{2,1},{3,2},{4,3},{5,4},{6,5},{7,6},{8,7},{9,8},{10,9},{11,1... | collective-permute-start | bytes 15368 | tf_op jit(solution)/shard_map/ppermute | solution.py:21
  396.3 6.2 collective-permute-start
  403.8 18.0 collective-permute-start.2
  405.7 16.1 collective-permute-start.3
  559.9 5.8 collective-permute-start
  567.1 18.0 collective-permute-start.2
  570.0 15.1 collective-permute-start.3
  723.5 6.0 collective-permute-start
  730.9 18.0 collective-permute-start.2
  733.6 15.3 collective-permute-start.3
  887.1 6.0 collective-permute-start
  894.4 18.0 collective-permute-start.2
  897.2 15.3 collective-permute-start.3
  1050.7 6.0 collective-permute-start
  1058.0 18.0 collective-permute-start.2
  1060.8 15.3 collective-permute-start.3
  1214.3 6.0 collective-permute-start
  1221.6 18.0 collective-permute-start.2
  1224.3 15.3 collective-permute-start.3
  1377.9 6.0 collective-permute-start
  1385.2 18.0 collective-permute-start.2
  1387.9 15.3 collective-permute-start.3
  1541.5 6.0 collective-permute-start
  1548.8 18.0 collective-permute-start.2
  1551.5 15.3 collective-permute-start.3
  1705.1 6.0 collective-permute-start
  1712.4 18.0 collective-permute-start.2
  1715.1 15.3 collective-permute-start.3
  1868.6 6.0 collective-permute-start
  1876.0 18.0 collective-permute-start.2
  1878.7 15.3 collective-permute-start.3
  2041.6 6.0 collective-permute-start.32
  2050.8 5.6 collective-permute-start.34
  2054.5 6.6 collective-permute-start.35
  2074.3 5.3 collective-permute-start.36
  2082.8 5.8 collective-permute-start.38
  2084.9 6.6 collective-permute-start.39
  2119.7 5.5 collective-permute-start.42
  2121.6 6.8 collective-permute-start.43
  2153.2 5.3 collective-permute-start.46
  2155.2 6.8 collective-permute-start.47
  (225 other events, 1486.9 us)
where the time goes:
time: 2180 us; the launch traced here: 2160 us
  blocking collectives  1320 us (61%)
  local copies, waits for them, and re-layouts  303 us (14%)
  starting transfers between devices  256 us (12%)
  other arithmetic  103 us (5%)
  matrix products  92.5 us (4%)
  waiting for transfers between devices  59.1 us (3%)
  loops' own time  22.8 us (1%)
    psum x21, blocking collectives, sum_spread(): return lax.psum(partial_sum, ('gx', 'gy'))  1320 us
    ppermute x42, starting transfers between devices, with_halo(): lax.ppermute(tail, axis, [(i, (i + 1) % count) for i in range(ends)])  150 us
    ppermute x42, starting transfers between devices, with_halo(): lax.ppermute(head, axis, [((i + 1) % count, i) for i in range(ends)])  106 us
    mul x58, local copies, waits for them, and re-layouts, spread_counts(): at_end * step_two[:, :, 2:][:, :, :, None]  67 us
    add x52, local copies, waits for them, and re-layouts, spread_counts(): step_two[:, :, 1:-1][:, :, :, None]  64.9 us
    mul x58, local copies, waits for them, and re-layouts, spread_counts(): at_start * step_two[:, :, :-2][:, :, :, None]  54.8 us
    ppermute x42, waiting for transfers between devices, with_halo(): lax.ppermute(head, axis, [((i + 1) % count, i) for i in range(ends)])  51.8 us
  transfers between devices with their start and end apart: 84, of which 26 were waited for; matrix products, arithmetic and copies ran while one was open for 11% of the time, Pallas kernels for 0%

commit v1 on v0

--- a/solution.py
+++ b/solution.py
@@ -297,7 +297,7 @@
 
 
 def sum_spread(partial_sum):
-    return lax.psum(partial_sum, ("gx", "gy"))
+    return lax.psum(lax.psum(partial_sum, "gx"), "gy")
 
 
 def coarse_spread(target, level_info):

time: 2180 us -> 1870 us (0.86)
  blocking collectives: 1320 us -> 944 us
  starting transfers between devices: 256 us -> 314 us
    psum x21 -> x42, blocking collectives: 1320 us -> 944 us  [sum_spread(): return lax.psum(lax.psum(partial_sum, 'gx'), 'gy')]
    ppermute x42, starting transfers between devices: 106 us -> 193 us  [with_halo(): lax.ppermute(head, axis, [((i + 1) % count, i) for i in range(ends)])]
    ppermute x42, starting transfers between devices: 150 us -> 121 us  [with_halo(): lax.ppermute(tail, axis, [(i, (i + 1) % count) for i in range(ends)])]
  transfers between devices with their start and end apart: 84 -> 84, of which waited for: 26 -> 28; matrix products, arithmetic and copies ran while one was open for 11% -> 12% of each run, Pallas kernels for 0% -> 0%
where the time goes in v1:
time: 1870 us; the launch traced here: 1850 us
  blocking collectives  944 us (50%)
  starting transfers between devices  314 us (17%)
  local copies, waits for them, and re-layouts  306 us (16%)
  other arithmetic  101 us (5%)
  matrix products  92.5 us (5%)
  waiting for transfers between devices  67.4 us (4%)
  loops' own time  22.2 us (1%)
    psum x42, blocking collectives, sum_spread(): return lax.psum(lax.psum(partial_sum, 'gx'), 'gy')  944 us
    ppermute x42, starting transfers between devices, with_halo(): lax.ppermute(head, axis, [((i + 1) % count, i) for i in range(ends)])  193 us
    ppermute x42, starting transfers between devices, with_halo(): lax.ppermute(tail, axis, [(i, (i + 1) % count) for i in range(ends)])  121 us
    mul x58, local copies, waits for them, and re-layouts, spread_counts(): at_end * step_two[:, :, 2:][:, :, :, None]  69.8 us
    add x52, local copies, waits for them, and re-layouts, spread_counts(): step_two[:, :, 1:-1][:, :, :, None]  66.9 us
    mul x58, local copies, waits for them, and re-layouts, spread_counts(): at_start * step_two[:, :, :-2][:, :, :, None]  57.4 us
    ppermute x42, waiting for transfers between devices, with_halo(): lax.ppermute(head, axis, [((i + 1) % count, i) for i in range(ends)])  56.1 us
  transfers between devices with their start and end apart: 84, of which 28 were waited for; matrix products, arithmetic and copies ran while one was open for 12% of the time, Pallas kernels for 0%

profile of v1, /device:TPU:105, one launch (start us, length us, event | category | flops | bytes accessed | tf_op | source)
XLA Modules:
  0.0 1851.9 jit_solution(631694189876199651)
XLA Ops:
  22.5 4.7 copy.272
  30.0 4.6 copy.273
  37.5 4.7 copy.275
  44.9 4.7 copy.281
  52.4 4.7 copy.282
  59.9 4.7 copy.284
  329.8 11.5 psum.54
  342.0 24.4 %psum.55 = f32[]{:T(128)} all-reduce(f32[]{:T(128)} %psum.54), channel_id=1, replica_groups=mesh['gx'=8,'gy'=16] {'gy'}, use_global_device_ids=true, to_apply=%region_2.3 | all-reduce | flops 1 | bytes 8 | tf_op jit(solution)/shard_map/psum | solution.py:300
  366.5 1342.1 %while.23 = (s32[]{:T(128)}, f32[8,8,128]{2,1,0:T(8,128)}, f32[8,8,128]{2,1,0:T(8,128)}, f32[8,8,128]{2,1,0:T(8,128)S(1)}, f32[]{:T(128)}, /*index=5*/f32[8,8,64...) while((s32[]{:T(128)}, f32[8,8,128]{2,1,0:T(8,128)}, ...), condition=%wide.region_10.11_spmd.clone.clone.clone.clone.clone, body=%wide.region_3.10_spmd.sunk.clone.clone.clone.clone.clone.sunk | while | flops 13401095 | bytes 2653811 | solution.py:293
  371.5 11.3 collective-permute-start
  388.4 5.5 collective-permute-start.3
  406.8 13.2 psum.84
  419.9 24.1 %psum.85 = f32[]{:T(128)} all-reduce(f32[]{:T(128)} %psum.84), channel_id=1, replica_groups=mesh['gx'=8,'gy'=16] {'gy'}, use_global_device_ids=true, to_apply=%region_6.6 | all-reduce | flops 1 | bytes 8 | tf_op jit(solution)/shard_map/while/body/eval_jaxpr/psum | solution.py:300
  446.7 20.0 %psum.86 = f32[]{:T(128)} all-reduce(f32[]{:T(128)} %get-tuple-element.825), channel_id=1, replica_groups=mesh['gx'=8,'gy'=16] {'gx'}, use_global_device_ids=true, to_apply=%region_8.8 | all-reduce | flops 1 | bytes 8 | tf_op jit(solution)/shard_map/while/body/eval_jaxpr/psum | solution.py:300
  466.7 28.1 %psum.87 = f32[]{:T(128)} all-reduce(f32[]{:T(128)} %psum.86), channel_id=1, replica_groups=mesh['gx'=8,'gy'=16] {'gy'}, use_global_device_ids=true, to_apply=%region_9.9 | all-reduce | flops 1 | bytes 8 | tf_op jit(solution)/shard_map/while/body/eval_jaxpr/psum | solution.py:300
  501.9 9.2 collective-permute-start
  535.0 13.2 psum.84
  548.2 28.9 %psum.85 = f32[]{:T(128)} all-reduce(f32[]{:T(128)} %psum.84), channel_id=1, replica_groups=mesh['gx'=8,'gy'=16] {'gy'}, use_global_device_ids=true, to_apply=%region_6.6 | all-reduce | flops 1 | bytes 8 | tf_op jit(solution)/shard_map/while/body/eval_jaxpr/psum | solution.py:300
  579.8 20.1 %psum.86 = f32[]{:T(128)} all-reduce(f32[]{:T(128)} %get-tuple-element.825), channel_id=1, replica_groups=mesh['gx'=8,'gy'=16] {'gx'}, use_global_device_ids=true, to_apply=%region_8.8 | all-reduce | flops 1 | bytes 8 | tf_op jit(solution)/shard_map/while/body/eval_jaxpr/psum | solution.py:300
  599.9 29.3 %psum.87 = f32[]{:T(128)} all-reduce(f32[]{:T(128)} %psum.86), channel_id=1, replica_groups=mesh['gx'=8,'gy'=16] {'gy'}, use_global_device_ids=true, to_apply=%region_9.9 | all-reduce | flops 1 | bytes 8 | tf_op jit(solution)/shard_map/while/body/eval_jaxpr/psum | solution.py:300
  636.3 9.5 collective-permute-start
  669.7 13.2 psum.84
  682.9 28.9 %psum.85 = f32[]{:T(128)} all-reduce(f32[]{:T(128)} %psum.84), channel_id=1, replica_groups=mesh['gx'=8,'gy'=16] {'gy'}, use_global_device_ids=true, to_apply=%region_6.6 | all-reduce | flops 1 | bytes 8 | tf_op jit(solution)/shard_map/while/body/eval_jaxpr/psum | solution.py:300
  714.4 20.1 %psum.86 = f32[]{:T(128)} all-reduce(f32[]{:T(128)} %get-tuple-element.825), channel_id=1, replica_groups=mesh['gx'=8,'gy'=16] {'gx'}, use_global_device_ids=true, to_apply=%region_8.8 | all-reduce | flops 1 | bytes 8 | tf_op jit(solution)/shard_map/while/body/eval_jaxpr/psum | solution.py:300
  734.6 29.3 %psum.87 = f32[]{:T(128)} all-reduce(f32[]{:T(128)} %psum.86), channel_id=1, replica_groups=mesh['gx'=8,'gy'=16] {'gy'}, use_global_device_ids=true, to_apply=%region_9.9 | all-reduce | flops 1 | bytes 8 | tf_op jit(solution)/shard_map/while/body/eval_jaxpr/psum | solution.py:300
  770.9 9.5 collective-permute-start
  804.4 13.2 psum.84
  817.6 28.9 %psum.85 = f32[]{:T(128)} all-reduce(f32[]{:T(128)} %psum.84), channel_id=1, replica_groups=mesh['gx'=8,'gy'=16] {'gy'}, use_global_device_ids=true, to_apply=%region_6.6 | all-reduce | flops 1 | bytes 8 | tf_op jit(solution)/shard_map/while/body/eval_jaxpr/psum | solution.py:300
  849.1 20.1 %psum.86 = f32[]{:T(128)} all-reduce(f32[]{:T(128)} %get-tuple-element.825), channel_id=1, replica_groups=mesh['gx'=8,'gy'=16] {'gx'}, use_global_device_ids=true, to_apply=%region_8.8 | all-reduce | flops 1 | bytes 8 | tf_op jit(solution)/shard_map/while/body/eval_jaxpr/psum | solution.py:300
  869.2 29.3 %psum.87 = f32[]{:T(128)} all-reduce(f32[]{:T(128)} %psum.86), channel_id=1, replica_groups=mesh['gx'=8,'gy'=16] {'gy'}, use_global_device_ids=true, to_apply=%region_9.9 | all-reduce | flops 1 | bytes 8 | tf_op jit(solution)/shard_map/while/body/eval_jaxpr/psum | solution.py:300
  905.6 9.5 collective-permute-start
  939.0 13.2 psum.84
  952.2 28.9 %psum.85 = f32[]{:T(128)} all-reduce(f32[]{:T(128)} %psum.84), channel_id=1, replica_groups=mesh['gx'=8,'gy'=16] {'gy'}, use_global_device_ids=true, to_apply=%region_6.6 | all-reduce | flops 1 | bytes 8 | tf_op jit(solution)/shard_map/while/body/eval_jaxpr/psum | solution.py:300
  983.8 20.1 %psum.86 = f32[]{:T(128)} all-reduce(f32[]{:T(128)} %get-tuple-element.825), channel_id=1, replica_groups=mesh['gx'=8,'gy'=16] {'gx'}, use_global_device_ids=true, to_apply=%region_8.8 | all-reduce | flops 1 | bytes 8 | tf_op jit(solution)/shard_map/while/body/eval_jaxpr/psum | solution.py:300
  1003.9 29.3 %psum.87 = f32[]{:T(128)} all-reduce(f32[]{:T(128)} %psum.86), channel_id=1, replica_groups=mesh['gx'=8,'gy'=16] {'gy'}, use_global_device_ids=true, to_apply=%region_9.9 | all-reduce | flops 1 | bytes 8 | tf_op jit(solution)/shard_map/while/body/eval_jaxpr/psum | solution.py:300
  1040.3 9.5 collective-permute-start
  1073.7 13.2 psum.84
  1086.9 28.9 %psum.85 = f32[]{:T(128)} all-reduce(f32[]{:T(128)} %psum.84), channel_id=1, replica_groups=mesh['gx'=8,'gy'=16] {'gy'}, use_global_device_ids=true, to_apply=%region_6.6 | all-reduce | flops 1 | bytes 8 | tf_op jit(solution)/shard_map/while/body/eval_jaxpr/psum | solution.py:300
  1118.4 20.1 %psum.86 = f32[]{:T(128)} all-reduce(f32[]{:T(128)} %get-tuple-element.825), channel_id=1, replica_groups=mesh['gx'=8,'gy'=16] {'gx'}, use_global_device_ids=true, to_apply=%region_8.8 | all-reduce | flops 1 | bytes 8 | tf_op jit(solution)/shard_map/while/body/eval_jaxpr/psum | solution.py:300
  1138.5 29.3 %psum.87 = f32[]{:T(128)} all-reduce(f32[]{:T(128)} %psum.86), channel_id=1, replica_groups=mesh['gx'=8,'gy'=16] {'gy'}, use_global_device_ids=true, to_apply=%region_9.9 | all-reduce | flops 1 | bytes 8 | tf_op jit(solution)/shard_map/while/body/eval_jaxpr/psum | solution.py:300
  1174.9 9.5 collective-permute-start
  1208.4 13.2 psum.84
  1221.5 28.9 %psum.85 = f32[]{:T(128)} all-reduce(f32[]{:T(128)} %psum.84), channel_id=1, replica_groups=mesh['gx'=8,'gy'=16] {'gy'}, use_global_device_ids=true, to_apply=%region_6.6 | all-reduce | flops 1 | bytes 8 | tf_op jit(solution)/shard_map/while/body/eval_jaxpr/psum | solution.py:300
  1253.1 20.1 %psum.86 = f32[]{:T(128)} all-reduce(f32[]{:T(128)} %get-tuple-element.825), channel_id=1, replica_groups=mesh['gx'=8,'gy'=16] {'gx'}, use_global_device_ids=true, to_apply=%region_8.8 | all-reduce | flops 1 | bytes 8 | tf_op jit(solution)/shard_map/while/body/eval_jaxpr/psum | solution.py:300
  1273.2 29.3 %psum.87 = f32[]{:T(128)} all-reduce(f32[]{:T(128)} %psum.86), channel_id=1, replica_groups=mesh['gx'=8,'gy'=16] {'gy'}, use_global_device_ids=true, to_apply=%region_9.9 | all-reduce | flops 1 | bytes 8 | tf_op jit(solution)/shard_map/while/body/eval_jaxpr/psum | solution.py:300
  1309.6 9.5 collective-permute-start
  1343.0 13.2 psum.84
  1356.2 28.9 %psum.85 = f32[]{:T(128)} all-reduce(f32[]{:T(128)} %psum.84), channel_id=1, replica_groups=mesh['gx'=8,'gy'=16] {'gy'}, use_global_device_ids=true, to_apply=%region_6.6 | all-reduce | flops 1 | bytes 8 | tf_op jit(solution)/shard_map/while/body/eval_jaxpr/psum | solution.py:300
  1387.8 20.1 %psum.86 = f32[]{:T(128)} all-reduce(f32[]{:T(128)} %get-tuple-element.825), channel_id=1, replica_groups=mesh['gx'=8,'gy'=16] {'gx'}, use_global_device_ids=true, to_apply=%region_8.8 | all-reduce | flops 1 | bytes 8 | tf_op jit(solution)/shard_map/while/body/eval_jaxpr/psum | solution.py:300
  1407.9 29.3 %psum.87 = f32[]{:T(128)} all-reduce(f32[]{:T(128)} %psum.86), channel_id=1, replica_groups=mesh['gx'=8,'gy'=16] {'gy'}, use_global_device_ids=true, to_apply=%region_9.9 | all-reduce | flops 1 | bytes 8 | tf_op jit(solution)/shard_map/while/body/eval_jaxpr/psum | solution.py:300
  1444.2 9.5 collective-permute-start
  1477.7 13.2 psum.84
  1490.9 28.9 %psum.85 = f32[]{:T(128)} all-reduce(f32[]{:T(128)} %psum.84), channel_id=1, replica_groups=mesh['gx'=8,'gy'=16] {'gy'}, use_global_device_ids=true, to_apply=%region_6.6 | all-reduce | flops 1 | bytes 8 | tf_op jit(solution)/shard_map/while/body/eval_jaxpr/psum | solution.py:300
  1522.4 20.1 %psum.86 = f32[]{:T(128)} all-reduce(f32[]{:T(128)} %get-tuple-element.825), channel_id=1, replica_groups=mesh['gx'=8,'gy'=16] {'gx'}, use_global_device_ids=true, to_apply=%region_8.8 | all-reduce | flops 1 | bytes 8 | tf_op jit(solution)/shard_map/while/body/eval_jaxpr/psum | solution.py:300
  1542.5 29.3 %psum.87 = f32[]{:T(128)} all-reduce(f32[]{:T(128)} %psum.86), channel_id=1, replica_groups=mesh['gx'=8,'gy'=16] {'gy'}, use_global_device_ids=true, to_apply=%region_9.9 | all-reduce | flops 1 | bytes 8 | tf_op jit(solution)/shard_map/while/body/eval_jaxpr/psum | solution.py:300
  1578.9 9.5 collective-permute-start
  1612.4 13.2 psum.84
  1625.5 28.9 %psum.85 = f32[]{:T(128)} all-reduce(f32[]{:T(128)} %psum.84), channel_id=1, replica_groups=mesh['gx'=8,'gy'=16] {'gy'}, use_global_device_ids=true, to_apply=%region_6.6 | all-reduce | flops 1 | bytes 8 | tf_op jit(solution)/shard_map/while/body/eval_jaxpr/psum | solution.py:300
  1657.1 20.1 %psum.86 = f32[]{:T(128)} all-reduce(f32[]{:T(128)} %get-tuple-element.825), channel_id=1, replica_groups=mesh['gx'=8,'gy'=16] {'gx'}, use_global_device_ids=true, to_apply=%region_8.8 | all-reduce | flops 1 | bytes 8 | tf_op jit(solution)/shard_map/while/body/eval_jaxpr/psum | solution.py:300
  1677.2 29.3 %psum.87 = f32[]{:T(128)} all-reduce(f32[]{:T(128)} %psum.86), channel_id=1, replica_groups=mesh['gx'=8,'gy'=16] {'gy'}, use_global_device_ids=true, to_apply=%region_9.9 | all-reduce | flops 1 | bytes 8 | tf_op jit(solution)/shard_map/while/body/eval_jaxpr/psum | solution.py:300
  1722.9 7.7 collective-permute-start.32
  1735.8 4.6 collective-permute-start.34
  1742.3 5.1 collective-permute-done.35
  1844.3 4.9 collective-permute-done.47
  (1198 shorter events, 728.4 us)
Async XLA Ops:
  2.9 9.5 collective-permute-start.4
  6.6 5.8 collective-permute-start.5
  13.1 59.8 %collective-permute-start.6 = (f32[26,1,384]{2,1,0:T(1,128)}, f32[26,1,384]{2,1,0:T(1,128)}, u32[]{:S(2)}, u32[]{:S(2)}) collective-permute-start(f32[26,1,384]{2,1,0:T(1,128)} %get-tuple-element.590), channel_id=1, source_target_pairs={{0,1},{1,2},{2,3},{3,4},{4,5},{5,6},{6,7},{7,8},{8,9},{9,10},{10,1... | collective-permute-start | bytes 119816 | tf_op jit(solution)/shard_map/ppermute | solution.py:19
  15.0 57.9 %collective-permute-start.7 = (f32[26,1,384]{2,1,0:T(1,128)}, f32[26,1,384]{2,1,0:T(1,128)}, u32[]{:S(2)}, u32[]{:S(2)}) collective-permute-start(f32[26,1,384]{2,1,0:T(1,128)} %get-tuple-element.591), channel_id=1, source_target_pairs={{1,0},{2,1},{3,2},{4,3},{5,4},{6,5},{7,6},{8,7},{9,8},{10,9},{11,1... | collective-permute-start | bytes 119816 | tf_op jit(solution)/shard_map/ppermute | solution.py:21
  93.2 6.2 collective-permute-start.8
  97.4 5.3 collective-permute-start.9
  102.8 7.0 collective-permute-start.10
  106.7 6.8 collective-permute-start.11
  129.4 6.4 collective-permute-start.12
  133.0 5.3 collective-permute-start.13
  138.3 6.2 collective-permute-start.14
  140.3 6.8 collective-permute-start.15
  170.2 55.3 %collective-permute-start.18 = (f32[18,1,256]{2,1,0:T(1,128)S(1)}, f32[18,1,256]{2,1,0:T(1,128)S(1)}, u32[]{:S(2)}, u32[]{:S(2)}) collective-permute-start(f32[18,1,256]{2,1,0:T(1,128)S(1)} %get-tuple-element.620), channel_id=1, source_target_pairs={{0,1},{1,2},{2,3},{3,4},{4,5},{5,6},{6,7},{7,8},{8,9},{9,10},{10,1... | collective-permute-start | bytes 55304 | tf_op jit(solution)/shard_map/ppermute | solution.py:19
  172.2 54.0 %collective-permute-start.19 = (f32[18,1,256]{2,1,0:T(1,128)S(1)}, f32[18,1,256]{2,1,0:T(1,128)}, u32[]{:S(2)}, u32[]{:S(2)}) collective-permute-start(f32[18,1,256]{2,1,0:T(1,128)S(1)} %get-tuple-element.621), channel_id=1, source_target_pairs={{1,0},{2,1},{3,2},{4,3},{5,4},{6,5},{7,6},{8,7},{9,8},{10,9},{11,1... | collective-permute-start | bytes 55304 | tf_op jit(solution)/shard_map/ppermute | solution.py:21
  242.5 5.7 collective-permute-start.20
  250.1 7.4 collective-permute-start.22
  254.1 6.6 collective-permute-start.23
  272.2 5.3 collective-permute-start.24
  280.7 6.1 collective-permute-start.26
  282.6 6.6 collective-permute-start.27
  293.1 5.7 collective-permute-start.28
  301.7 24.5 %collective-permute-start.30 = (f32[10,1,128]{2,1,0:T(1,128)}, f32[10,1,128]{2,1,0:T(1,128)}, u32[]{:S(2)}, u32[]{:S(2)}) collective-permute-start(f32[10,1,128]{2,1,0:T(1,128)} %get-tuple-element.666), channel_id=1, source_target_pairs={{0,1},{1,2},{2,3},{3,4},{4,5},{5,6},{6,7},{7,8},{8,9},{9,10},{10,1... | collective-permute-start | bytes 15368 | tf_op jit(solution)/shard_map/ppermute | solution.py:19
  303.6 22.6 %collective-permute-start.31 = (f32[10,1,128]{2,1,0:T(1,128)}, f32[10,1,128]{2,1,0:T(1,128)}, u32[]{:S(2)}, u32[]{:S(2)}) collective-permute-start(f32[10,1,128]{2,1,0:T(1,128)} %get-tuple-element.667), channel_id=1, source_target_pairs={{1,0},{2,1},{3,2},{4,3},{5,4},{6,5},{7,6},{8,7},{9,8},{10,9},{11,1... | collective-permute-start | bytes 15368 | tf_op jit(solution)/shard_map/ppermute | solution.py:21
  371.5 13.3 collective-permute-start
  386.5 18.0 collective-permute-start.2
  388.4 16.0 collective-permute-start.3
  501.9 11.1 collective-permute-start
  514.8 18.0 collective-permute-start.2
  519.2 13.5 collective-permute-start.3
  636.3 11.4 collective-permute-start
  649.4 18.0 collective-permute-start.2
  653.9 13.5 collective-permute-start.3
  770.9 11.4 collective-permute-start
  784.1 18.0 collective-permute-start.2
  788.6 13.5 collective-permute-start.3
  905.6 11.4 collective-permute-start
  918.8 18.0 collective-permute-start.2
  923.2 13.5 collective-permute-start.3
  1040.3 11.4 collective-permute-start
  1053.4 18.0 collective-permute-start.2
  1057.9 13.5 collective-permute-start.3
  1174.9 11.4 collective-permute-start
  1188.1 18.0 collective-permute-start.2
  1192.5 13.5 collective-permute-start.3
  1309.6 11.4 collective-permute-start
  1322.7 18.0 collective-permute-start.2
  1327.2 13.5 collective-permute-start.3
  1444.2 11.4 collective-permute-start
  1457.4 18.0 collective-permute-start.2
  1461.9 13.5 collective-permute-start.3
  1578.9 11.4 collective-permute-start
  1592.1 18.0 collective-permute-start.2
  1596.5 13.5 collective-permute-start.3
  1722.9 10.8 collective-permute-start.32
  1735.8 6.5 collective-permute-start.34
  1740.4 7.1 collective-permute-start.35
  1768.7 5.8 collective-permute-start.38
  1770.8 6.6 collective-permute-start.39
  1800.2 5.3 collective-permute-start.41
  1805.6 5.5 collective-permute-start.42
  1807.5 6.8 collective-permute-start.43
  1833.6 5.3 collective-permute-start.45
  1838.9 5.3 collective-permute-start.46
  1842.3 6.8 collective-permute-start.47
  (250 other events, 1686.9 us)
